TPU v7x, 256 devices: a whole 4x4x8 slice. The times are simulated.
256 devices in a mesh: dp: 16 (over y_lo, x, core), seq: 16 (over z, y_hi).
Axes of the slice: x: 4, y: 4 (y_hi: 2, y_lo: 2; y = y_hi * 2 + y_lo), z: 8, core: 2. Of those that a mesh axis runs over, the one named last changes fastest.
Arguments:
- primal: bfloat16 [16, 2048, 3, 4096], P('dp', 'seq'), as said below
- tangent: bfloat16 [16, 2048, 3, 4096], P('dp', 'seq'), may hold values from -6 to 6
- cotangent: bfloat16 [16, 2048, 2560], P('dp', 'seq'), may hold values from -6 to 6
Outputs:
- attended: bfloat16 [16, 2048, 4096], P('dp', 'seq')
- attended_tangent: bfloat16 [16, 2048, 4096], P('dp', 'seq')
- weight_grad: float32 [2560, 4096], P('dp', 'seq')
Inputs may be any that keep to these rules, and one draw needn't show every extreme that they name: `primal`: slots 0, 1, 2 of the third dimension are queries, keys and values.
All inputs are finite; a program needn't handle non-finite values.
Results may differ from a plain program's by a relative error of at most 0.005.
Values may be sent and summed in bfloat16 or wider, within the bound.
A program may use at most 128 MiB of HBM per device.

v0:
```python
import jax
import jax.numpy as jnp
from jax import lax
from jax.sharding import PartitionSpec as P

HEAD_DIM = 128


def block_jvp(query_block, dquery_block, keys, dkeys, values, dvalues):
    scale = 1.0 / HEAD_DIM**0.5
    scores = (
        jnp.einsum("qhd,khd->hqk", query_block, keys, preferred_element_type=jnp.float32) * scale
    )
    top = jnp.max(scores, axis=-1, keepdims=True)
    expo = jnp.exp(scores - top)
    probs = expo / jnp.sum(expo, axis=-1, keepdims=True)
    probs_low = probs.astype(jnp.bfloat16)
    out = jnp.einsum("hqk,khd->qhd", probs_low, values, preferred_element_type=jnp.float32)
    dscores = jnp.einsum("qhd,khd->hqk", dquery_block, keys, preferred_element_type=jnp.float32)
    dscores = (
        dscores + jnp.einsum("qhd,khd->hqk", query_block, dkeys, preferred_element_type=jnp.float32)
    ) * scale
    centre = jnp.sum(probs * dscores, axis=-1, keepdims=True)
    dprobs = (probs * (dscores - centre)).astype(jnp.bfloat16)
    dout = jnp.einsum("hqk,khd->qhd", probs_low, dvalues, preferred_element_type=jnp.float32)
    dout = dout + jnp.einsum("hqk,khd->qhd", dprobs, values, preferred_element_type=jnp.float32)
    return (out.astype(jnp.bfloat16), dout.astype(jnp.bfloat16))


def body(primal, tangent, cotangent):
    prim_heads, tang_heads = (
        lax.all_to_all(primal, "seq", split_axis=3, concat_axis=1, tiled=True),
        lax.all_to_all(tangent, "seq", split_axis=3, concat_axis=1, tiled=True),
    )
    seq_len = prim_heads.shape[1]
    local_width = prim_heads.shape[3]
    head_count = local_width // HEAD_DIM
    prim_heads = prim_heads[0].reshape(seq_len, 3, head_count, HEAD_DIM)
    tang_heads = tang_heads[0].reshape(seq_len, 3, head_count, HEAD_DIM)
    keys, values = (prim_heads[:, 1], prim_heads[:, 2])
    dkeys, dvalues = (tang_heads[:, 1], tang_heads[:, 2])
    block = min(512, seq_len)
    queries = prim_heads[:, 0].reshape(seq_len // block, block, head_count, HEAD_DIM)
    dqueries = tang_heads[:, 0].reshape(seq_len // block, block, head_count, HEAD_DIM)

    def one_block(pair):
        return block_jvp(pair[0], pair[1], keys, dkeys, values, dvalues)

    outs, douts = lax.map(one_block, (queries, dqueries))
    outs = outs.reshape(1, seq_len, local_width)
    douts = douts.reshape(1, seq_len, local_width)
    attended, attended_tangent = (
        lax.all_to_all(outs, "seq", split_axis=1, concat_axis=2, tiled=True),
        lax.all_to_all(douts, "seq", split_axis=1, concat_axis=2, tiled=True),
    )
    full_cot = lax.all_gather(cotangent, "seq", axis=1, tiled=True)[0]
    heads_out = outs[0]
    term = lax.dot_general(
        full_cot, heads_out, (((0,), (0,)), ((), ())), preferred_element_type=jnp.float32
    )
    weight_grad = lax.psum_scatter(term, "dp", scatter_dimension=0, tiled=True)
    return (attended, attended_tangent, weight_grad)


def solution(mesh):
    return jax.shard_map(
        body,
        mesh=mesh,
        in_specs=(P("dp", "seq", None, None), P("dp", "seq", None, None), P("dp", "seq", None)),
        out_specs=(P("dp", "seq", None), P("dp", "seq", None), P("dp", "seq")),
        check_vma=False,
    )
```

profile of v0, /device:TPU:47, one launch (start us, length us, event | category | flops | bytes accessed | tf_op | source)
XLA Modules:
  0.0 473.9 jit_solution(12705735730795649485)
XLA Ops:
  7.2 7.3 %copy.42 = bf16[1,128,3,4096]{1,2,0,3:T(4,128)(2,1)} copy(bf16[1,128,3,4096]{3,1,2,0:T(8,128)(2,1)} %param.6) | data formatting | bytes 6291456 | tf_op args[1]
  14.5 9.8 %all-to-all-start.1 = ((bf16[1,128,3,4096]{1,2,0,3:T(4,128)(2,1)}), bf16[1,128,3,4096]{1,2,0,3:T(4,128)(2,1)}, u32[]{:S(2)}, u32[]{:S(2)}) async-start(bf16[1,128,3,4096]{1,2,0,3:T(4,128)(2,1)} %copy.42), calls=%async_computation.1 | async-start | bytes 8388608 | tf_op jit(solution)/shard_map/all_to_all | solution.py:33
  24.2 4.8 %copy.39 = bf16[1,128,3,4096]{1,2,0,3:T(4,128)(2,1)} copy(bf16[1,128,3,4096]{3,1,2,0:T(8,128)(2,1)S(1)} %copy-done.3) | data formatting | bytes 6291456 | tf_op args[0]
  29.0 89.3 %all-to-all-done.1 = bf16[1,128,3,4096]{1,2,0,3:T(4,128)(2,1)} async-done(((bf16[1,128,3,4096]{1,2,0,3:T(4,128)(2,1)}), bf16[1,128,3,4096]{1,2,0,3:T(4,128)(2,1)}, u32[]{:S(2)}, u32[]{:S(2)}) %all-to-all-start.1) | async-done | bytes 3145760 | tf_op jit(solution)/shard_map/all_to_all | solution.py:33
  118.3 8.9 %all-to-all-start = ((bf16[1,128,3,4096]{1,2,0,3:T(4,128)(2,1)}), bf16[1,128,3,4096]{1,2,0,3:T(4,128)(2,1)}, u32[]{:S(2)}, u32[]{:S(2)}) async-start(bf16[1,128,3,4096]{1,2,0,3:T(4,128)(2,1)} %copy.39), calls=%async_computation | async-start | bytes 8388608 | tf_op jit(solution)/shard_map/all_to_all | solution.py:32
  128.0 4.8 %copy.80 = bf16[1,128,3,16,256]{1,3,4,2,0:T(8,128)(2,1)S(1)} copy(bf16[1,128,3,16,256]{1,2,4,3,0:T(4,128)(2,1)} %bitcast.11) | data formatting | bytes 6291456 | tf_op jit(solution)/shard_map/all_to_all | solution.py:33
  132.8 3.3 reshape_squeeze.14
  136.1 3.5 slice_bitcast_fusion
  141.0 105.0 %all-to-all-done = bf16[1,128,3,4096]{1,2,0,3:T(4,128)(2,1)} async-done(((bf16[1,128,3,4096]{1,2,0,3:T(4,128)(2,1)}), bf16[1,128,3,4096]{1,2,0,3:T(4,128)(2,1)}, u32[]{:S(2)}, u32[]{:S(2)}) %all-to-all-start) | async-done | bytes 3145760 | tf_op jit(solution)/shard_map/all_to_all | solution.py:32
  245.9 4.8 %copy.81 = bf16[1,128,3,16,256]{1,3,4,2,0:T(8,128)(2,1)S(1)} copy(bf16[1,128,3,16,256]{1,2,4,3,0:T(4,128)(2,1)} %bitcast.6) | data formatting | bytes 6291456 | tf_op jit(solution)/shard_map/all_to_all | solution.py:32
  250.7 3.4 reshape_squeeze.12
  254.1 3.7 slice_bitcast_fusion.2
  259.0 1.7 copy.46
  260.7 2.3 copy.47
  263.0 2.3 copy.48
  266.6 99.2 %while.12 = (s32[]{:T(128)}, bf16[4,512,2,128]{3,2,1,0:T(2,128)(2,1)S(1)}, bf16[4,512,2,128]{3,2,1,0:T(2,128)(2,1)}, bf16[4,512,2,128]{3,1,0,2:T(8,128)(2,1)}, b...) while((s32[]{:T(128)}, ...), condition=%wide.region_4.5_spmd, body=%wide.region_0.4_spmd.sunk | while | flops 3255174144 | bytes 131365072 | solution.py:49
  266.6 6.9 %fusion.95 = (f32[2,512]{1,0:T(2,128)S(1)}, f32[2,512,2048]{2,1,0:T(8,128)}) fusion(bf16[2048,2,128]{2,0,1:T(8,128)(2,1)S(1)} %get-tuple-element.213, bf16[4,512,2,128]{3,1,0,2:T(8,128)(2,1)} %get-tuple-element.212, s32[]{:T(128)} %get-tuple-element.199), kind=kOutput, calls=%fused_computation.49.clone.1 | convolution fusion | flops 543164416 | bytes 9703936 | tf_op jit(solution)/shard_map/while/body/eval_jaxpr/sub | solution.py:15
  273.5 2.4 fusion.96
  275.8 1.5 copy-done.7
  277.3 5.5 %multiply_reduce_fusion.3 = (f32[2,512]{1,0:T(2,128)S(1)}, f32[2,512,2048]{2,1,0:T(8,128)}) fusion(f32[2,512,2048]{2,1,0:T(8,128)S(1)} %copy-done.7, f32[2,512]{1,0:T(2,128)S(1)} %get-tuple-element.184, f32[2,512,2048]{2,1,0:T(8,128)S(1)} %fusion.96, bf16[2048,2,128]{2,0,1:T(8,128)(2,1)S(1)} %copy-done.6, ...), kind=kOutput, calls=%fused_computation.2.clone.1 | convolution fusion | flops 547355648 | bytes 26485248 | tf_op jit(solution)/shard_map/while/body/eval_jaxpr/qhd,khd->hqk/dot_general | solution.py:21
  282.8 4.5 fusion.97
  291.4 6.9 %fusion.95 = (f32[2,512]{1,0:T(2,128)S(1)}, f32[2,512,2048]{2,1,0:T(8,128)}) fusion(bf16[2048,2,128]{2,0,1:T(8,128)(2,1)S(1)} %get-tuple-element.213, bf16[4,512,2,128]{3,1,0,2:T(8,128)(2,1)} %get-tuple-element.212, s32[]{:T(128)} %get-tuple-element.199), kind=kOutput, calls=%fused_computation.49.clone.1 | convolution fusion | flops 543164416 | bytes 9703936 | tf_op jit(solution)/shard_map/while/body/eval_jaxpr/sub | solution.py:15
  298.2 2.3 fusion.96
  300.6 1.4 copy-done.7
  302.0 5.5 %multiply_reduce_fusion.3 = (f32[2,512]{1,0:T(2,128)S(1)}, f32[2,512,2048]{2,1,0:T(8,128)}) fusion(f32[2,512,2048]{2,1,0:T(8,128)S(1)} %copy-done.7, f32[2,512]{1,0:T(2,128)S(1)} %get-tuple-element.184, f32[2,512,2048]{2,1,0:T(8,128)S(1)} %fusion.96, bf16[2048,2,128]{2,0,1:T(8,128)(2,1)S(1)} %copy-done.6, ...), kind=kOutput, calls=%fused_computation.2.clone.1 | convolution fusion | flops 547355648 | bytes 26485248 | tf_op jit(solution)/shard_map/while/body/eval_jaxpr/qhd,khd->hqk/dot_general | solution.py:21
  307.5 4.5 fusion.97
  316.1 6.9 %fusion.95 = (f32[2,512]{1,0:T(2,128)S(1)}, f32[2,512,2048]{2,1,0:T(8,128)}) fusion(bf16[2048,2,128]{2,0,1:T(8,128)(2,1)S(1)} %get-tuple-element.213, bf16[4,512,2,128]{3,1,0,2:T(8,128)(2,1)} %get-tuple-element.212, s32[]{:T(128)} %get-tuple-element.199), kind=kOutput, calls=%fused_computation.49.clone.1 | convolution fusion | flops 543164416 | bytes 9703936 | tf_op jit(solution)/shard_map/while/body/eval_jaxpr/sub | solution.py:15
  323.0 2.4 fusion.96
  325.4 1.5 copy-done.7
  326.9 5.5 %multiply_reduce_fusion.3 = (f32[2,512]{1,0:T(2,128)S(1)}, f32[2,512,2048]{2,1,0:T(8,128)}) fusion(f32[2,512,2048]{2,1,0:T(8,128)S(1)} %copy-done.7, f32[2,512]{1,0:T(2,128)S(1)} %get-tuple-element.184, f32[2,512,2048]{2,1,0:T(8,128)S(1)} %fusion.96, bf16[2048,2,128]{2,0,1:T(8,128)(2,1)S(1)} %copy-done.6, ...), kind=kOutput, calls=%fused_computation.2.clone.1 | convolution fusion | flops 547355648 | bytes 26485248 | tf_op jit(solution)/shard_map/while/body/eval_jaxpr/qhd,khd->hqk/dot_general | solution.py:21
  332.4 4.6 fusion.97
  341.1 6.9 %fusion.95 = (f32[2,512]{1,0:T(2,128)S(1)}, f32[2,512,2048]{2,1,0:T(8,128)}) fusion(bf16[2048,2,128]{2,0,1:T(8,128)(2,1)S(1)} %get-tuple-element.213, bf16[4,512,2,128]{3,1,0,2:T(8,128)(2,1)} %get-tuple-element.212, s32[]{:T(128)} %get-tuple-element.199), kind=kOutput, calls=%fused_computation.49.clone.1 | convolution fusion | flops 543164416 | bytes 9703936 | tf_op jit(solution)/shard_map/while/body/eval_jaxpr/sub | solution.py:15
  348.0 2.4 fusion.96
  350.3 1.4 copy-done.7
  351.8 5.5 %multiply_reduce_fusion.3 = (f32[2,512]{1,0:T(2,128)S(1)}, f32[2,512,2048]{2,1,0:T(8,128)}) fusion(f32[2,512,2048]{2,1,0:T(8,128)S(1)} %copy-done.7, f32[2,512]{1,0:T(2,128)S(1)} %get-tuple-element.184, f32[2,512,2048]{2,1,0:T(8,128)S(1)} %fusion.96, bf16[2048,2,128]{2,0,1:T(8,128)(2,1)S(1)} %copy-done.6, ...), kind=kOutput, calls=%fused_computation.2.clone.1 | convolution fusion | flops 547355648 | bytes 26485248 | tf_op jit(solution)/shard_map/while/body/eval_jaxpr/qhd,khd->hqk/dot_general | solution.py:21
  357.2 4.5 fusion.97
  366.8 5.9 %fusion.53 = f32[2560,256]{0,1:T(8,128)S(1)} fusion(bf16[1,2048,2560]{2,1,0:T(8,128)(2,1)} %all-gather.2.cloned.1.call-done, bf16[256,8,2,128]{3,2,1,0:T(2,128)(2,1)} %bitcast.118), kind=kOutput, calls=%fused_computation.40 | convolution fusion | flops 2684354560 | bytes 14155776 | tf_op jit(solution)/shard_map/dot_general | solution.py:58
  372.7 2.1 copy.61
  374.9 6.4 %reshape.19 = bf16[1,2048,256]{2,0,1:T(2,128)(2,1)S(1)} reshape(bf16[4,512,2,128]{3,2,1,0:T(2,128)(2,1)} %copy-done.1) | data formatting | bytes 2097152 | tf_op jit(solution)/shard_map/reshape | solution.py:50
  381.8 10.7 %reduce = bf16[2048,256]{1,0:T(8,128)(2,1)S(1)} reduce(bf16[2048,1,256]{2,1,0:T(2,128)(2,1)S(1)} %bitcast.116, bf16[]{:T(256)} %broadcast.18), dimensions={1}, to_apply=%bitcast.71.reduce_sub_computation | reduce | bytes 2097154
  393.6 7.1 %all-to-all-start.2 = ((bf16[16,2,16384]{2,1,0:T(2,128)(2,1)}), bf16[16,2,16384]{2,1,0:T(2,128)(2,1)S(1)}, u32[]{:S(2)}, u32[]{:S(2)}) async-start(bf16[16,2,16384]{2,1,0:T(2,128)(2,1)} %reshape.23), calls=%async_computation.2 | async-start | bytes 2097152 | tf_op jit(solution)/shard_map/all_to_all | solution.py:53
  400.8 6.4 %reshape.20 = bf16[1,2048,256]{2,0,1:T(2,128)(2,1)S(1)} reshape(bf16[4,512,2,128]{3,2,1,0:T(2,128)(2,1)} %get-tuple-element.52) | data formatting | bytes 2097152 | tf_op jit(solution)/shard_map/reshape | solution.py:51
  407.1 11.5 %reduce.1 = bf16[2048,256]{1,0:T(8,128)(2,1)} reduce(bf16[2048,1,256]{2,1,0:T(2,128)(2,1)S(1)} %bitcast.117, bf16[]{:T(256)} %broadcast.18), dimensions={1}, to_apply=%bitcast.73.reduce_sub_computation | reduce | bytes 2097154
  418.6 2.2 reshape.25
  420.8 7.4 %all-to-all-done.2 = bf16[16,2,16384]{2,1,0:T(2,128)(2,1)S(1)} async-done(((bf16[16,2,16384]{2,1,0:T(2,128)(2,1)}), bf16[16,2,16384]{2,1,0:T(2,128)(2,1)S(1)}, u32[]{:S(2)}, u32[]{:S(2)}) %all-to-all-start.2) | async-done | bytes 1048608 | tf_op jit(solution)/shard_map/all_to_all | solution.py:53
  428.2 5.7 %all-to-all-start.3 = ((bf16[16,2,16384]{2,1,0:T(2,128)(2,1)}), bf16[16,2,16384]{2,1,0:T(2,128)(2,1)}, u32[]{:S(2)}, u32[]{:S(2)}) async-start(bf16[16,2,16384]{2,1,0:T(2,128)(2,1)} %reshape.25), calls=%async_computation.3 | async-start | bytes 2097152 | tf_op jit(solution)/shard_map/all_to_all | solution.py:54
  437.2 23.4 %all-to-all-done.3 = bf16[16,2,16384]{2,1,0:T(2,128)(2,1)} async-done(((bf16[16,2,16384]{2,1,0:T(2,128)(2,1)}), bf16[16,2,16384]{2,1,0:T(2,128)(2,1)}, u32[]{:S(2)}, u32[]{:S(2)}) %all-to-all-start.3) | async-done | bytes 1048608 | tf_op jit(solution)/shard_map/all_to_all | solution.py:54
  460.6 4.3 reshape.26
  (68 shorter events, 28.7 us)
Async XLA Ops:
  7.2 17.1 %copy-start.3 = (bf16[1,128,3,4096]{3,1,2,0:T(8,128)(2,1)S(1)}, bf16[1,128,3,4096]{3,1,2,0:T(8,128)(2,1)}, u32[]{:S(2)}) copy-start(bf16[1,128,3,4096]{3,1,2,0:T(8,128)(2,1)} %param.5) | copy-start | bytes 9437188
  14.5 103.8 %all-to-all-start.1 = ((bf16[1,128,3,4096]{1,2,0,3:T(4,128)(2,1)}), bf16[1,128,3,4096]{1,2,0,3:T(4,128)(2,1)}, u32[]{:S(2)}, u32[]{:S(2)}) async-start(bf16[1,128,3,4096]{1,2,0,3:T(4,128)(2,1)} %copy.42), calls=%async_computation.1 | async-start | bytes 8388608 | tf_op jit(solution)/shard_map/all_to_all | solution.py:33
  118.3 127.6 %all-to-all-start = ((bf16[1,128,3,4096]{1,2,0,3:T(4,128)(2,1)}), bf16[1,128,3,4096]{1,2,0,3:T(4,128)(2,1)}, u32[]{:S(2)}, u32[]{:S(2)}) async-start(bf16[1,128,3,4096]{1,2,0,3:T(4,128)(2,1)} %copy.39), calls=%async_computation | async-start | bytes 8388608 | tf_op jit(solution)/shard_map/all_to_all | solution.py:32
  127.2 238.6 %all-gather.2.cloned.1.call-start = ((), (), s32[]{:S(2)}) async-start(), calls=%async_computation.5 | async-start | bytes 11141120 | tf_op jit(solution)/shard_map/all_gather | solution.py:56
  128.0 339.1 %reduce-scatter.4.cloned.1.call-start = ((), (), s32[]{:S(2)}) async-start(), calls=%async_computation.6 | async-start | bytes 2785280
  254.1 11.2 %copy-start.2 = (bf16[2048,2,128]{0,2,1:T(8,128)(2,1)S(1)}, bf16[2048,2,128]{0,2,1:T(8,128)(2,1)}, u32[]{:S(2)}) copy-start(bf16[2048,2,128]{0,2,1:T(8,128)(2,1)} %get-tuple-element.116) | copy-start | bytes 3145732
  254.1 12.5 %copy-start = (bf16[4,512,2,128]{3,2,1,0:T(2,128)(2,1)S(1)}, bf16[4,512,2,128]{3,2,1,0:T(2,128)(2,1)}, u32[]{:S(2)}) copy-start(bf16[4,512,2,128]{3,2,1,0:T(2,128)(2,1)} %custom-call) | copy-start | bytes 3145732
  273.5 2.4 copy-start.6
  273.5 3.8 copy-start.7
  277.3 5.5 %copy-start.4 = (bf16[2048,2,128]{2,0,1:T(8,128)(2,1)S(1)}, bf16[2048,2,128]{2,0,1:T(8,128)(2,1)}, u32[]{:S(2)}) copy-start(bf16[2048,2,128]{2,0,1:T(8,128)(2,1)} %get-tuple-element.214) | copy-start | bytes 3145732 | tf_op jit(solution)/shard_map/while
  282.8 4.5 copy-start.5
  298.2 2.4 copy-start.6
  298.2 3.8 copy-start.7
  302.0 5.5 %copy-start.4 = (bf16[2048,2,128]{2,0,1:T(8,128)(2,1)S(1)}, bf16[2048,2,128]{2,0,1:T(8,128)(2,1)}, u32[]{:S(2)}) copy-start(bf16[2048,2,128]{2,0,1:T(8,128)(2,1)} %get-tuple-element.214) | copy-start | bytes 3145732 | tf_op jit(solution)/shard_map/while
  307.5 4.5 copy-start.5
  323.0 2.4 copy-start.6
  323.0 3.9 copy-start.7
  326.9 5.5 %copy-start.4 = (bf16[2048,2,128]{2,0,1:T(8,128)(2,1)S(1)}, bf16[2048,2,128]{2,0,1:T(8,128)(2,1)}, u32[]{:S(2)}) copy-start(bf16[2048,2,128]{2,0,1:T(8,128)(2,1)} %get-tuple-element.214) | copy-start | bytes 3145732 | tf_op jit(solution)/shard_map/while
  332.4 4.6 copy-start.5
  348.0 2.4 copy-start.6
  348.0 3.8 copy-start.7
  351.8 5.5 %copy-start.4 = (bf16[2048,2,128]{2,0,1:T(8,128)(2,1)S(1)}, bf16[2048,2,128]{2,0,1:T(8,128)(2,1)}, u32[]{:S(2)}) copy-start(bf16[2048,2,128]{2,0,1:T(8,128)(2,1)} %get-tuple-element.214) | copy-start | bytes 3145732 | tf_op jit(solution)/shard_map/while
  357.2 4.5 copy-start.5
  365.8 1.0 copy-start.1
  393.6 34.6 %all-to-all-start.2 = ((bf16[16,2,16384]{2,1,0:T(2,128)(2,1)}), bf16[16,2,16384]{2,1,0:T(2,128)(2,1)S(1)}, u32[]{:S(2)}, u32[]{:S(2)}) async-start(bf16[16,2,16384]{2,1,0:T(2,128)(2,1)} %reshape.23), calls=%async_computation.2 | async-start | bytes 2097152 | tf_op jit(solution)/shard_map/all_to_all | solution.py:53
  428.2 32.3 %all-to-all-start.3 = ((bf16[16,2,16384]{2,1,0:T(2,128)(2,1)}), bf16[16,2,16384]{2,1,0:T(2,128)(2,1)}, u32[]{:S(2)}, u32[]{:S(2)}) async-start(bf16[16,2,16384]{2,1,0:T(2,128)(2,1)} %reshape.25), calls=%async_computation.3 | async-start | bytes 2097152 | tf_op jit(solution)/shard_map/all_to_all | solution.py:54
Sparse Core Ops, SparseCore 0:
  130.6 222.4 all-gather.1
  375.0 66.4 reduce-scatter.3
where the time goes:
time: 480 us; the launch traced here: 474 us
  waiting for transfers between devices  226 us (47%)
  matrix products  94.1 us (20%)
  local copies, waits for them, and re-layouts  85.9 us (18%)
  starting transfers between devices  31.6 us (7%)
  other arithmetic  22.3 us (5%)
  between operations  14.2 us (3%)
    all_to_all x1, waiting for transfers between devices, body(): lax.all_to_all(primal, 'seq', split_axis=3, concat_axis=1, tiled=True)  105 us
    all_to_all x1, waiting for transfers between devices, body(): lax.all_to_all(tangent, 'seq', split_axis=3, concat_axis=1, tiled=True)  89.3 us
    sub x4, matrix products, block_jvp(): expo = jnp.exp(scores - top)  27.5 us
    unnamed x20, local copies, waits for them, and re-layouts  27.3 us
    all_to_all x1, waiting for transfers between devices, body(): lax.all_to_all(douts, 'seq', split_axis=1, concat_axis=2, tiled=True)  23.4 us
    unnamed x2, other arithmetic  22.2 us
    dot_general x4, matrix products, block_jvp(): jnp.einsum('qhd,khd->hqk', query_block, dkeys, preferred_element_type=jnp...  22 us
    dot_general x4, matrix products, block_jvp(): jnp.einsum('hqk,khd->qhd', dprobs, values, preferred_element_type=jnp.flo...  18.2 us
  transfers between devices with their start and end apart: 6, of which 4 were waited for; matrix products, arithmetic and copies ran while one was open for 38% of the time, Pallas kernels for 0%

commit v1 on v0

v1 whole, which is shorter than its diff:
```python
import jax
import jax.numpy as jnp
from jax import lax
from jax.experimental import pallas as pl
from jax.experimental.pallas import tpu as pltpu
from jax.sharding import PartitionSpec as P

MESH = pl.DeviceIdType.MESH
HEAD_DIM = 128
TOKENS = 128
SEQ_LEN = 2048
WIDTH = 4096
FEATURES = 2560
HALF = FEATURES // 2
ROWS = 160
NSEQ = 16
NDP = 16
NZ = 8
LOCAL_HEADS = 2
BLOCK = 256
BLOCKS = SEQ_LEN // BLOCK
SCALE = 1.0 / HEAD_DIM**0.5


def wait_bytes(ref, sem):
    pltpu.make_async_copy(ref, ref, sem).wait()


def kernel(
    prim, tang, cot, att_out, tan_out, wg_out,
    qkv, cots, own, own_t, part, term, terms,
    qkv_send, qkv_recv, cot_send, cot_recv, cot_local,
    out_send, att_recv, tan_recv, part_send, part_recv, term_send, term_recv,
):
    dp, seq = lax.axis_index("dp"), lax.axis_index("seq")
    z, yh = seq // 2, seq % 2
    yl = dp // 8
    partner = seq + 1 - 2 * yh
    up, down = lax.rem(z + 1, NZ) * 2 + yh, lax.rem(z + NZ - 1, NZ) * 2 + yh
    mine = yl == yh

    barrier = pltpu.get_barrier_semaphore()

    def greet_seq(o, c):
        pl.semaphore_signal(
            barrier, inc=1, device_id=(dp, lax.rem(seq + o, NSEQ)), device_id_type=MESH
        )
        return c

    lax.fori_loop(1, NSEQ, greet_seq, 0)

    def greet_dp(i, c):
        @pl.when(jnp.logical_or(i != dp, jnp.logical_not(mine)))
        def _():
            pl.semaphore_signal(
                barrier, inc=1, device_id=(i, z * 2 + yl), device_id_type=MESH
            )

        return c

    lax.fori_loop(0, NDP, greet_dp, 0)

    @pl.when(mine)
    def _():
        pl.semaphore_wait(barrier, NSEQ - 1 + NDP - 1)

    @pl.when(jnp.logical_not(mine))
    def _():
        pl.semaphore_wait(barrier, NSEQ - 1 + NDP)

    def rows_of(device):
        return pl.ds(pl.multiple_of(device * TOKENS, TOKENS), TOKENS)

    def send_qkv(h):
        for a, array in enumerate((prim, tang)):
            pltpu.make_async_copy(
                array.at[:, :, pl.ds(pl.multiple_of(seq * 256 + h * 128, 128), 128)],
                qkv.at[h, :, rows_of(seq), pl.ds(a * 128, 128)],
                qkv_recv.at[h],
            ).start()

        def one(o, c):
            to = lax.rem(seq + o, NSEQ)
            for a, array in enumerate((prim, tang)):
                pltpu.make_async_remote_copy(
                    array.at[:, :, pl.ds(pl.multiple_of(to * 256 + h * 128, 128), 128)],
                    qkv.at[h, :, rows_of(seq), pl.ds(a * 128, 128)],
                    qkv_send.at[h],
                    qkv_recv.at[h],
                    device_id=(dp, to),
                    device_id_type=MESH,
                ).start()
            return c

        lax.fori_loop(1, NSEQ, one, 0)

    def half(which):
        return pl.ds(pl.multiple_of(which * HALF, HALF), HALF)

    send_qkv(0)
    to_partner = pltpu.make_async_remote_copy(
        cot.at[:, half(1 - yh)], cots.at[rows_of(seq)], cot_send.at[14], cot_recv.at[14],
        device_id=(dp, partner), device_id_type=MESH,
    )
    to_partner.start()
    local = pltpu.make_async_copy(cot.at[:, half(yh)], cots.at[rows_of(seq)], cot_local)
    local.start()

    def ring_copy(ring, way, step):
        source = lax.rem(z + (step if way else NZ - step), NZ) * 2
        source = source + (1 - yh if ring else yh)
        index = ring * 7 + (step + steps[ring, 0] if way else step)
        return pltpu.make_async_remote_copy(
            cots.at[rows_of(source)], cots.at[rows_of(source)],
            cot_send.at[index], cot_recv.at[index],
            device_id=(dp, down if way else up), device_id_type=MESH,
        )

    steps = {(0, 0): 4, (0, 1): 3, (1, 0): 3, (1, 1): 4}
    local.wait()
    copies = []
    for step in range(4):
        for ring in (0, 1):
            if step == 0 and ring == 1:
                send_qkv(1)
                to_partner.wait()
            for way in (0, 1):
                if step < steps[ring, way]:
                    if step:
                        ring_copy(ring, way, step - 1).wait_recv()
                    copy = ring_copy(ring, way, step)
                    copy.start()
                    copies.append((copy, step == steps[ring, way] - 1))
    for copy, last in copies:
        copy.wait_send()
        if last:
            copy.wait_recv()

    def attend(h):
        def one(step, carry):
            even = lax.rem(step, 2) == 0
            b = lax.rem(z + jnp.where(even, 4 - step // 2, 5 + step // 2), NZ)
            rows = pl.ds(pl.multiple_of(b * BLOCK, BLOCK), BLOCK)
            q = qkv[h, 0, rows, :]
            query, dquery = q[:, :HEAD_DIM], q[:, HEAD_DIM:]
            contract = (((1,), (1,)), ((), ()))
            scores = lax.dot_general(
                query, qkv[h, 1, :, :HEAD_DIM], contract, preferred_element_type=jnp.float32
            )
            dscores = lax.dot_general(
                jnp.concatenate([dquery, query], axis=1), qkv[h, 1], contract,
                preferred_element_type=jnp.float32,
            ) * SCALE
            top = jnp.max(scores, axis=-1, keepdims=True)
            expo = jnp.exp((scores - top) * SCALE)
            probs = expo * (1.0 / jnp.sum(expo, axis=-1, keepdims=True))
            centre = jnp.sum(probs * dscores, axis=-1, keepdims=True)
            dprobs = (probs * (dscores - centre)).astype(jnp.bfloat16)
            both = jnp.dot(
                probs.astype(jnp.bfloat16), qkv[h, 2], preferred_element_type=jnp.float32
            )
            dout = both[:, HEAD_DIM:] + jnp.dot(
                dprobs, qkv[h, 2, :, :HEAD_DIM], preferred_element_type=jnp.float32
            )
            own[h, rows, :] = both[:, :HEAD_DIM].astype(jnp.bfloat16)
            own_t[h, rows, :] = dout.astype(jnp.bfloat16)

            columns = pl.ds(pl.multiple_of(seq * 256 + h * 128, 128), 128)
            for y in (0, 1):
                to = b * 2 + y

                @pl.when(to != seq)
                def _():
                    for source, target, recv in (
                        (own, att_out, att_recv), (own_t, tan_out, tan_recv)
                    ):
                        pltpu.make_async_remote_copy(
                            source.at[h, rows_of(to)], target.at[:, columns],
                            out_send, recv, device_id=(dp, to), device_id_type=MESH,
                        ).start()

                @pl.when(to == seq)
                def _():
                    for source, target, recv in (
                        (own, att_out, att_recv), (own_t, tan_out, tan_recv)
                    ):
                        pltpu.make_async_copy(
                            source.at[h, rows_of(to)], target.at[:, columns], recv
                        ).start()

            pltpu.make_async_remote_copy(
                own.at[h, rows], part.at[h, rows], part_send.at[h], part_recv.at[h],
                device_id=(dp, partner), device_id_type=MESH,
            ).start()
            return carry

        lax.fori_loop(0, BLOCKS, one, 0)

    def weigh(h):
        wait_bytes(part.at[h], part_recv.at[h])
        both = jnp.concatenate([own[h], part[h]], axis=1)

        def one(n, carry):
            span = pl.ds(pl.multiple_of(n * 256, 256), 256)
            term[h, span, :] = lax.dot_general(
                cots[:, span], both, (((0,), (0,)), ((), ())),
                preferred_element_type=jnp.float32,
            )
            return carry

        lax.fori_loop(0, HALF // 256, one, 0)

        def send(n, carry):
            block = pl.ds(pl.multiple_of(n * ROWS, ROWS), ROWS)
            to = yh * 8 + n
            is_mine = jnp.logical_and(mine, to == dp)

            @pl.when(is_mine)
            def _():
                pltpu.make_async_copy(
                    term.at[h, block, pl.ds(0, 128)], terms.at[h, dp], term_recv.at[h]
                ).start()

            @pl.when(jnp.logical_not(is_mine))
            def _():
                pltpu.make_async_remote_copy(
                    term.at[h, block, pl.ds(0, 128)], terms.at[h, dp],
                    term_send.at[h], term_recv.at[h],
                    device_id=(to, seq), device_id_type=MESH,
                ).start()

            pltpu.make_async_remote_copy(
                term.at[h, block, pl.ds(128, 128)], terms.at[h, dp],
                term_send.at[h], term_recv.at[h],
                device_id=(to, partner), device_id_type=MESH,
            ).start()
            return carry

        lax.fori_loop(0, 8, send, 0)

    for h in range(LOCAL_HEADS):
        wait_bytes(qkv.at[h], qkv_recv.at[h])
        attend(h)
        weigh(h)

    for h in range(LOCAL_HEADS):
        wait_bytes(terms.at[h], term_recv.at[h])
        total = terms[h, 0]
        for s in range(1, NDP):
            total = total + terms[h, s]
        wg_out[:, pl.ds(h * 128, 128)] = total

    wait_bytes(att_out, att_recv)
    wait_bytes(tan_out, tan_recv)
    sent = pl.ds(0, (NSEQ - 1) * TOKENS)
    for h in range(LOCAL_HEADS):
        wait_bytes(qkv.at[h, :, sent], qkv_send.at[h])
        wait_bytes(part.at[h], part_send.at[h])

        @pl.when(mine)
        def _():
            wait_bytes(terms.at[h, pl.ds(0, NDP - 1)], term_send.at[h])

        @pl.when(jnp.logical_not(mine))
        def _():
            wait_bytes(terms.at[h], term_send.at[h])

    wait_bytes(qkv.at[:, 0, sent], out_send)


def body(primal, tangent, cotangent):
    prim = jnp.transpose(primal[0], (1, 0, 2))
    tang = jnp.transpose(tangent[0], (1, 0, 2))
    hbm = pl.BlockSpec(memory_space=pl.ANY)
    dma = pltpu.SemaphoreType.DMA
    bf16, f32 = jnp.bfloat16, jnp.float32
    att, tan, wg = pl.pallas_call(
        kernel,
        out_shape=(
            jax.ShapeDtypeStruct((TOKENS, WIDTH), bf16),
            jax.ShapeDtypeStruct((TOKENS, WIDTH), bf16),
            jax.ShapeDtypeStruct((ROWS, 256), f32),
        ),
        in_specs=[hbm] * 3,
        out_specs=(hbm, hbm, pl.BlockSpec(memory_space=pltpu.VMEM)),
        scratch_shapes=[
            pltpu.VMEM((LOCAL_HEADS, 3, SEQ_LEN, 256), bf16),
            pltpu.VMEM((SEQ_LEN, HALF), bf16),
            pltpu.VMEM((LOCAL_HEADS, SEQ_LEN, HEAD_DIM), bf16),
            pltpu.VMEM((LOCAL_HEADS, SEQ_LEN, HEAD_DIM), bf16),
            pltpu.VMEM((LOCAL_HEADS, SEQ_LEN, HEAD_DIM), bf16),
            pltpu.VMEM((LOCAL_HEADS, HALF, 256), f32),
            pltpu.VMEM((LOCAL_HEADS, NDP, ROWS, HEAD_DIM), f32),
            dma((2,)), dma((2,)), dma((15,)), dma((15,)), dma(()),
            dma(()), dma(()), dma(()), dma((2,)), dma((2,)), dma((2,)), dma((2,)),
        ],
        compiler_params=pltpu.CompilerParams(
            collective_id=0, has_side_effects=True, vmem_limit_bytes=56 * 2**20
        ),
        cost_estimate=pl.CostEstimate(
            flops=2 * 2 * SEQ_LEN * SEQ_LEN * 128 * 6 + 2 * FEATURES * 256 * SEQ_LEN,
            bytes_accessed=16 * 2**20, transcendentals=2 * SEQ_LEN * SEQ_LEN,
        ),
        name="attention_jvp",
    )(prim, tang, cotangent[0])
    return att[None], tan[None], wg


def solution(mesh):
    return jax.shard_map(
        body,
        mesh=mesh,
        in_specs=(P("dp", "seq", None, None), P("dp", "seq", None, None), P("dp", "seq", None)),
        out_specs=(P("dp", "seq", None), P("dp", "seq", None), P("dp", "seq")),
        check_vma=False,
    )
```

time: 480 us -> 326 us (0.68); the launches traced: 474 us -> 325 us
  Pallas kernels: 0 us -> 320 us
  waiting for transfers between devices: 226 us -> 0 us
  matrix products: 94.1 us -> 0 us
  local copies, waits for them, and re-layouts: 85.9 us -> 5.28 us
  starting transfers between devices: 31.6 us -> 0 us
  other arithmetic: 22.3 us -> 0 us
  between operations: 14.2 us -> 0.65 us
    pallas_call x0 -> x1, Pallas kernels: none -> 320 us  [body(): pl.pallas_call(kernel, out_shape=(jax.ShapeDtypeStruct((TOKENS, WIDTH), b...]
    all_to_all x4 -> x0, waiting for transfers between devices: 225 us -> none  [the longest x1 105 us: body(): lax.all_to_all(primal, 'seq', split_axis=3, concat_axis=1, tiled=True)]
    dot_general x21 -> x0, matrix products: 66.6 us -> none  [the longest x4 22 us: block_jvp(): jnp.einsum('qhd,khd->hqk', query_block, dkeys, preferred_element_type=jnp...]
    all_to_all x4 -> x0, starting transfers between devices: 31.6 us -> none  [the longest x1 9.76 us: body(): lax.all_to_all(tangent, 'seq', split_axis=3, concat_axis=1, tiled=True)]
    sub x4 -> x0, matrix products: 27.5 us -> none  [block_jvp(): expo = jnp.exp(scores - top)]
    unnamed x2 -> x0, other arithmetic: 22.2 us -> none
    unnamed x20 -> x5, local copies, waits for them, and re-layouts: 27.3 us -> 5.28 us
    while x36 -> x0, local copies, waits for them, and re-layouts: 13.5 us -> none  [the longest x4 7.56 us: body(): outs, douts = lax.map(one_block, (queries, dqueries))]
  transfers between devices with their start and end apart: 6 -> 0, of which waited for: 4 -> 0; matrix products, arithmetic and copies ran while one was open for 38% -> 0% of each run, Pallas kernels for 0% -> 0%
where the time goes in v1:
time: 326 us; the launch traced here: 325 us
  Pallas kernels  320 us (98%)
  local copies, waits for them, and re-layouts  5.28 us (2%)
    pallas_call x1, Pallas kernels, body(): pl.pallas_call(kernel, out_shape=(jax.ShapeDtypeStruct((TOKENS, WIDTH), b...  320 us

profile of v1, /device:TPU:47, one launch (start us, length us, event | category | flops | bytes accessed | tf_op | source)
XLA Modules:
  0.0 325.5 jit_solution(395027038314531786)
XLA Ops:
  0.6 319.6 %attention_jvp.1 = (bf16[128,4096]{1,0:T(8,128)(2,1)}, bf16[128,4096]{1,0:T(8,128)(2,1)}, f32[160,256]{1,0:T(8,128)}) custom-call(bf16[3,128,4096]{2,1,0:T(8,128)(2,1)} %bitcast.11, bf16[3,128,4096]{2,1,0:T(8,128)(2,1)} %bitcast.12, bf16[128,2560]{1,0:T(8,128)(2,1)} %bitcast.13), custom_call_target="tpu_custom_call" | custom-call | flops 15569256448 | bytes 16777216 | tf_op jit(solution)/shard_map/attention_jvp/pallas_call | solution.py:277
  320.2 0.0 copy-start
  320.2 2.3 copy.9
  322.5 2.3 copy.10
  324.8 0.0 copy-done
  324.8 0.7 copy.11
Async XLA Ops:
  320.2 4.6 %copy-start = (f32[160,256]{1,0:T(8,128)S(1)}, f32[160,256]{1,0:T(8,128)}, u32[]{:S(2)}) copy-start(f32[160,256]{1,0:T(8,128)} %get-tuple-element.14) | copy-start | bytes 491524

commit v2 on v1

v2 whole, which is shorter than its diff:
```python
import jax
import jax.numpy as jnp
from jax import lax
from jax.experimental import pallas as pl
from jax.experimental.pallas import tpu as pltpu
from jax.sharding import PartitionSpec as P

MESH = pl.DeviceIdType.MESH
HEAD_DIM = 128
TOKENS = 128
SEQ_LEN = 2048
WIDTH = 4096
FEATURES = 2560
QUARTER = FEATURES // 4
ROWS = 160
NSEQ = 16
NDP = 16
PLANE = 32
PLANE_TOKENS = PLANE * TOKENS
NZ = 8
LOCAL_HEADS = 2
BLOCK = 256
BLOCKS = SEQ_LEN // BLOCK
SCALE = 1.0 / HEAD_DIM**0.5


def wait_bytes(ref, sem):
    pltpu.make_async_copy(ref, ref, sem).wait()


def kernel(
    prim, tang, cot, att_out, tan_out, wg_out,
    qkv, cots, own, own_t, atts, term, terms,
    qkv_send, qkv_recv, cot_send, cot_recv, out_send, att_recv, tan_recv,
    spread_send, spread_recv, core_send, core_recv, term_send, term_recv,
):
    dp, seq = lax.axis_index("dp"), lax.axis_index("seq")
    z, yh = seq // 2, seq % 2
    yl, x, c = dp // 8, (dp // 2) % 4, dp % 2
    here = dp * 2 + yh
    mine = jnp.logical_and(x == 0, c == 0)

    def columns_at(x_at, way):
        apart = jnp.where(x_at == 0, 4, NZ - x_at)
        return jnp.where(way == 0, x_at, apart)

    def summed_at(offset):
        near = jnp.where(offset > 4, NZ - offset, offset)
        return lax.rem(near, 4)

    def rows_of(device):
        return pl.ds(pl.multiple_of(device * TOKENS, TOKENS), TOKENS)

    def head_columns(device, h):
        return pl.ds(pl.multiple_of(device * 256 + h * 128, 128), 128)

    barrier = pltpu.get_barrier_semaphore()

    def greet(dp_to, seq_to):
        pl.semaphore_signal(barrier, inc=1, device_id=(dp_to, seq_to), device_id_type=MESH)

    def greet_clip(o, carry):
        greet(dp, lax.rem(seq + o, NSEQ))
        return carry

    def greet_plane(o, carry):
        there = lax.rem(here + o, PLANE)
        greet(there // 2, z * 2 + there % 2)
        return carry

    def greet_terms(o, carry):
        source_dp = (yl * 4 + summed_at(o)) * 2 + x // 2

        @pl.when(jnp.logical_not(jnp.logical_and(mine, o == 0)))
        def _():
            greet(source_dp, lax.rem(z + NZ - o, NZ) * 2 + yh)

        return carry

    lax.fori_loop(1, NSEQ, greet_clip, 0)
    lax.fori_loop(1, PLANE, greet_plane, 0)
    lax.fori_loop(0, NZ, greet_terms, 0)

    @pl.when(mine)
    def _():
        pl.semaphore_wait(barrier, NSEQ - 1 + PLANE - 1 + NZ - 1)

    @pl.when(jnp.logical_not(mine))
    def _():
        pl.semaphore_wait(barrier, NSEQ - 1 + PLANE - 1 + NZ)

    def send_qkv(h, o):
        to = lax.rem(seq + o, NSEQ)
        for a, array in enumerate((prim, tang)):
            pltpu.make_async_remote_copy(
                array.at[:, :, head_columns(to, h)],
                qkv.at[h, :, rows_of(seq), pl.ds(a * 128, 128)],
                qkv_send.at[h],
                qkv_recv.at[h],
                device_id=(dp, to),
                device_id_type=MESH,
            ).start()

    def keep_qkv(h):
        for a, array in enumerate((prim, tang)):
            pltpu.make_async_copy(
                array.at[:, :, head_columns(seq, h)],
                qkv.at[h, :, rows_of(seq), pl.ds(a * 128, 128)],
                qkv_recv.at[h],
            ).start()

    place = c * 16 + (dp // 2) * 2 + yh

    def quarter(dp_to):
        return pl.ds(pl.multiple_of((dp_to // 8 * 2 + dp_to % 2) * QUARTER, 128), QUARTER)

    def send_cot(o):
        there = lax.rem(here + o, PLANE)
        pltpu.make_async_remote_copy(
            cot.at[:, quarter(there // 2)],
            cots.at[rows_of(place)],
            cot_send,
            cot_recv,
            device_id=(there // 2, z * 2 + there % 2),
            device_id_type=MESH,
        ).start()

    def first(o, carry):
        send_qkv(0, o)
        return carry

    def second(o, carry):
        send_qkv(1, o)
        send_cot(2 * o)
        send_cot(2 * o + 1)
        return carry

    keep_qkv(0)
    lax.fori_loop(1, NSEQ, first, 0)
    send_cot(1)
    lax.fori_loop(1, NSEQ, second, 0)
    keep_qkv(1)
    pltpu.make_async_copy(cot.at[:, quarter(dp)], cots.at[rows_of(place)], cot_recv).start()

    def attend(h, between):
        def one(step, carry):
            even = lax.rem(step, 2) == 0
            b = lax.rem(z + jnp.where(even, 4 - step // 2, 5 + step // 2), NZ)
            rows = pl.ds(pl.multiple_of(b * BLOCK, BLOCK), BLOCK)
            q = qkv[h, 0, rows, :]
            query, dquery = q[:, :HEAD_DIM], q[:, HEAD_DIM:]
            contract = (((1,), (1,)), ((), ()))
            scores = lax.dot_general(
                query, qkv[h, 1, :, :HEAD_DIM], contract, preferred_element_type=jnp.float32
            )
            dscores = lax.dot_general(
                jnp.concatenate([dquery, query], axis=1), qkv[h, 1], contract,
                preferred_element_type=jnp.float32,
            ) * SCALE
            top = jnp.max(scores, axis=-1, keepdims=True)
            expo = jnp.exp((scores - top) * SCALE)
            probs = expo * (1.0 / jnp.sum(expo, axis=-1, keepdims=True))
            centre = jnp.sum(probs * dscores, axis=-1, keepdims=True)
            dprobs = (probs * (dscores - centre)).astype(jnp.bfloat16)
            both = jnp.dot(
                probs.astype(jnp.bfloat16), qkv[h, 2], preferred_element_type=jnp.float32
            )
            dout = both[:, HEAD_DIM:] + jnp.dot(
                dprobs, qkv[h, 2, :, :HEAD_DIM], preferred_element_type=jnp.float32
            )
            own[h, rows, :] = both[:, :HEAD_DIM].astype(jnp.bfloat16)
            own_t[h, rows, :] = dout.astype(jnp.bfloat16)

            for source, target, recv in (
                (own, att_out, att_recv.at[h, seq]), (own_t, tan_out, tan_recv)
            ):
                for y in (0, 1):
                    to = b * 2 + y

                    @pl.when(to != seq)
                    def _():
                        pltpu.make_async_remote_copy(
                            source.at[h, rows_of(to)], target.at[:, head_columns(seq, h)],
                            out_send, recv, device_id=(dp, to), device_id_type=MESH,
                        ).start()

                    @pl.when(to == seq)
                    def _():
                        pltpu.make_async_copy(
                            source.at[h, rows_of(to)], target.at[:, head_columns(seq, h)], recv
                        ).start()

            for at, what in between:
                @pl.when(step == at)
                def _():
                    what()

            return carry

        lax.fori_loop(0, BLOCKS, one, 0)

    def spread(h):
        def one(o, carry):
            step = o // 2
            down = jnp.where(lax.rem(step, 2) == 0, 4 - step // 2, 5 + step // 2)
            source = lax.rem(z + NZ - down, NZ) * 2 + lax.rem(o, 2)
            offset = lax.rem(source // 2 - z + NZ, NZ)
            x_to, way = summed_at(offset), offset // 4
            wait_bytes(att_out.at[:, head_columns(source, h)], att_recv.at[h, source])
            lanes = pl.ds(pl.multiple_of(way * 128, 128), 128)
            for yl_to in (0, 1):
                dp_to = (yl_to * 4 + x_to) * 2 + c
                seq_to = z * 2 + source % 2
                is_here = jnp.logical_and(dp_to == dp, seq_to == seq)

                @pl.when(is_here)
                def _():
                    pltpu.make_async_copy(
                        att_out.at[:, head_columns(source, h)],
                        atts.at[h, rows_of(place), lanes], spread_recv.at[h],
                    ).start()

                @pl.when(jnp.logical_not(is_here))
                def _():
                    pltpu.make_async_remote_copy(
                        att_out.at[:, head_columns(source, h)],
                        atts.at[h, rows_of(place), lanes],
                        spread_send.at[h], spread_recv.at[h],
                        device_id=(dp_to, seq_to), device_id_type=MESH,
                    ).start()

            return carry

        lax.fori_loop(0, NSEQ, one, 0)

    def core_rows(core):
        return pl.ds(pl.multiple_of(core * (PLANE_TOKENS // 2), 128), PLANE_TOKENS // 2)

    def exchange(h):
        wait_bytes(atts.at[h, core_rows(c)], spread_recv.at[h])
        pltpu.make_async_remote_copy(
            atts.at[h, core_rows(c)], atts.at[h, core_rows(c)], core_send.at[h],
            core_recv.at[h], device_id=(dp + 1 - 2 * c, seq), device_id_type=MESH,
        ).start()

    def weigh(h):
        wait_bytes(atts.at[h, core_rows(1 - c)], core_recv.at[h])
        span = 1024

        def one(n, carry):
            tokens = pl.ds(pl.multiple_of(n * span, span), span)
            product = lax.dot_general(
                cots[tokens, :], atts[h, tokens, :], (((0,), (0,)), ((), ())),
                preferred_element_type=jnp.float32,
            )
            term[h] = jnp.where(n == 0, product, term[h] + product)
            return carry

        lax.fori_loop(0, PLANE_TOKENS // span, one, 0)

        def send(n, carry):
            block = pl.ds(pl.multiple_of(n * ROWS, ROWS), ROWS)
            dp_to = (yl * 4 + 2 * c + n // 2) * 2 + n % 2
            for way in (0, 1):
                seq_to = lax.rem(z + columns_at(x, way), NZ) * 2 + yh
                source = term.at[h, block, pl.ds(way * 128, 128)]

                def away():
                    pltpu.make_async_remote_copy(
                        source, terms.at[h, z], term_send.at[h], term_recv.at[h],
                        device_id=(dp_to, seq_to), device_id_type=MESH,
                    ).start()

                if way:
                    away()
                else:
                    is_mine = jnp.logical_and(mine, n == 0)
                    pl.when(jnp.logical_not(is_mine))(away)

                    @pl.when(is_mine)
                    def _():
                        pltpu.make_async_copy(source, terms.at[h, z], term_recv.at[h]).start()

            return carry

        lax.fori_loop(0, 4, send, 0)

    def total(h):
        wait_bytes(terms.at[h], term_recv.at[h])
        result = terms[h, 0]
        for s in range(1, NZ):
            result = result + terms[h, s]
        wg_out[:, pl.ds(h * 128, 128)] = result

    wait_bytes(qkv.at[0], qkv_recv.at[0])
    attend(0, ())
    wait_bytes(qkv.at[1], qkv_recv.at[1])
    attend(1, ((4, lambda: spread(0)), (6, lambda: exchange(0))))
    spread(1)
    wait_bytes(cots, cot_recv)
    weigh(0)
    exchange(1)
    weigh(1)
    total(0)
    total(1)

    wait_bytes(tan_out, tan_recv)
    sent = pl.ds(0, (NSEQ - 1) * TOKENS)
    wait_bytes(cots.at[pl.ds(0, (PLANE - 1) * TOKENS)], cot_send)
    for h in range(LOCAL_HEADS):
        wait_bytes(qkv.at[h, :, sent], qkv_send.at[h])
        wait_bytes(atts.at[h, pl.ds(0, 15 * TOKENS)], spread_send.at[h])
        wait_bytes(atts.at[h, core_rows(c)], core_send.at[h])

        @pl.when(mine)
        def _():
            wait_bytes(terms.at[h, pl.ds(0, NZ - 1)], term_send.at[h])

        @pl.when(jnp.logical_not(mine))
        def _():
            wait_bytes(terms.at[h], term_send.at[h])

    wait_bytes(qkv.at[:, 0, sent], out_send)


def body(primal, tangent, cotangent):
    prim = jnp.transpose(primal[0], (1, 0, 2))
    tang = jnp.transpose(tangent[0], (1, 0, 2))
    hbm = pl.BlockSpec(memory_space=pl.ANY)
    dma = pltpu.SemaphoreType.DMA
    bf16, f32 = jnp.bfloat16, jnp.float32
    att, tan, wg = pl.pallas_call(
        kernel,
        out_shape=(
            jax.ShapeDtypeStruct((TOKENS, WIDTH), bf16),
            jax.ShapeDtypeStruct((TOKENS, WIDTH), bf16),
            jax.ShapeDtypeStruct((ROWS, 256), f32),
        ),
        in_specs=[hbm] * 3,
        out_specs=(hbm, hbm, pl.BlockSpec(memory_space=pltpu.VMEM)),
        scratch_shapes=[
            pltpu.VMEM((LOCAL_HEADS, 3, SEQ_LEN, 256), bf16),
            pltpu.VMEM((PLANE_TOKENS, QUARTER), bf16),
            pltpu.VMEM((LOCAL_HEADS, SEQ_LEN, HEAD_DIM), bf16),
            pltpu.VMEM((LOCAL_HEADS, SEQ_LEN, HEAD_DIM), bf16),
            pltpu.VMEM((LOCAL_HEADS, PLANE_TOKENS, 256), bf16),
            pltpu.VMEM((LOCAL_HEADS, QUARTER, 256), f32),
            pltpu.VMEM((LOCAL_HEADS, NZ, ROWS, HEAD_DIM), f32),
            dma((2,)), dma((2,)), dma(()), dma(()), dma(()), dma((2, NSEQ)), dma(()),
            dma((2,)), dma((2,)), dma((2,)), dma((2,)), dma((2,)), dma((2,)),
        ],
        compiler_params=pltpu.CompilerParams(
            collective_id=0, has_side_effects=True, vmem_limit_bytes=56 * 2**20
        ),
        cost_estimate=pl.CostEstimate(
            flops=2 * 2 * SEQ_LEN * SEQ_LEN * 128 * 6 + 2 * FEATURES * 256 * SEQ_LEN,
            bytes_accessed=16 * 2**20, transcendentals=2 * SEQ_LEN * SEQ_LEN,
        ),
        name="attention_jvp",
    )(prim, tang, cotangent[0])
    return att[None], tan[None], wg


def solution(mesh):
    return jax.shard_map(
        body,
        mesh=mesh,
        in_specs=(P("dp", "seq", None, None), P("dp", "seq", None, None), P("dp", "seq", None)),
        out_specs=(P("dp", "seq", None), P("dp", "seq", None), P("dp", "seq")),
        check_vma=False,
    )
```

time: 326 us -> 290 us (0.89); the launches traced: 325 us -> 285 us
  Pallas kernels: 320 us -> 279 us
    pallas_call x1, Pallas kernels: 320 us -> 279 us  [body(): pl.pallas_call(kernel, out_shape=(jax.ShapeDtypeStruct((TOKENS, WIDTH), b...]
where the time goes in v2:
time: 290 us; the launch traced here: 285 us
  Pallas kernels  279 us (96%)
  local copies, waits for them, and re-layouts  5.28 us (2%)
    pallas_call x1, Pallas kernels, body(): pl.pallas_call(kernel, out_shape=(jax.ShapeDtypeStruct((TOKENS, WIDTH), b...  279 us

profile of v2, /device:TPU:47, one launch (start us, length us, event | category | flops | bytes accessed | tf_op | source)
XLA Modules:
  0.0 284.6 jit_solution(6219557964716892097)
XLA Ops:
  0.6 278.6 %attention_jvp.1 = (bf16[128,4096]{1,0:T(8,128)(2,1)}, bf16[128,4096]{1,0:T(8,128)(2,1)}, f32[160,256]{1,0:T(8,128)}) custom-call(bf16[3,128,4096]{2,1,0:T(8,128)(2,1)} %bitcast.11, bf16[3,128,4096]{2,1,0:T(8,128)(2,1)} %bitcast.12, bf16[128,2560]{1,0:T(8,128)(2,1)} %bitcast.13), custom_call_target="tpu_custom_call" | custom-call | flops 15569256448 | bytes 16777216 | tf_op jit(solution)/shard_map/attention_jvp/pallas_call | solution.py:332
  279.3 0.0 copy-start
  279.3 2.3 copy.9
  281.6 2.3 copy.10
  283.9 0.0 copy-done
  283.9 0.7 copy.11
Async XLA Ops:
  279.3 4.6 %copy-start = (f32[160,256]{1,0:T(8,128)S(1)}, f32[160,256]{1,0:T(8,128)}, u32[]{:S(2)}) copy-start(f32[160,256]{1,0:T(8,128)} %get-tuple-element.14) | copy-start | bytes 491524

commit v3 on v2

--- a/solution.py
+++ b/solution.py
@@ -30,7 +30,7 @@
 
 def kernel(
     prim, tang, cot, att_out, tan_out, wg_out,
-    qkv, cots, own, own_t, atts, term, terms,
+    qkv, cots, own, own_t, stats, atts, total_of, term, terms,
     qkv_send, qkv_recv, cot_send, cot_recv, out_send, att_recv, tan_recv,
     spread_send, spread_recv, core_send, core_recv, term_send, term_recv,
 ):
@@ -109,21 +109,44 @@
                 qkv_recv.at[h],
             ).start()
 
-    place = c * 16 + (dp // 2) * 2 + yh
+    place = x * 8 + yh * 4 + yl * 2 + c
 
     def quarter(dp_to):
         return pl.ds(pl.multiple_of((dp_to // 8 * 2 + dp_to % 2) * QUARTER, 128), QUARTER)
 
-    def send_cot(o):
-        there = lax.rem(here + o, PLANE)
+    def tokens_at(first, places):
+        return pl.ds(pl.multiple_of(first * TOKENS, TOKENS), places * TOKENS)
+
+    same_y, same_x = tokens_at(x * 8 + yh * 4, 4), tokens_at(x * 8, 8)
+
+    def cot_quarters():
+        for n in range(1, 4):
+            dp_to = (lax.rem(yl + n // 2, 2) * 4 + x) * 2 + lax.rem(c + n % 2, 2)
+            pltpu.make_async_remote_copy(
+                cot.at[:, quarter(dp_to)], cots.at[rows_of(place)],
+                cot_send.at[n - 1], cot_recv.at[n - 1],
+                device_id=(dp_to, seq), device_id_type=MESH,
+            ).start()
+        pltpu.make_async_copy(
+            cot.at[:, quarter(dp)], cots.at[rows_of(place)], cot_recv.at[3]
+        ).start()
+
+    def cot_along_y():
+        for n in range(4):
+            wait_bytes(cots.at[rows_of(place)], cot_recv.at[n])
         pltpu.make_async_remote_copy(
-            cot.at[:, quarter(there // 2)],
-            cots.at[rows_of(place)],
-            cot_send,
-            cot_recv,
-            device_id=(there // 2, z * 2 + there % 2),
-            device_id_type=MESH,
+            cots.at[same_y], cots.at[same_y], cot_send.at[3], cot_recv.at[4],
+            device_id=(dp, z * 2 + 1 - yh), device_id_type=MESH,
         ).start()
+
+    def cot_along_x():
+        wait_bytes(cots.at[same_y], cot_recv.at[4])
+        for n in range(1, 4):
+            dp_to = (yl * 4 + lax.rem(x + n, 4)) * 2 + c
+            pltpu.make_async_remote_copy(
+                cots.at[same_x], cots.at[same_x], cot_send.at[3 + n], cot_recv.at[4 + n],
+                device_id=(dp_to, seq), device_id_type=MESH,
+            ).start()
 
     def first(o, carry):
         send_qkv(0, o)
@@ -131,73 +154,110 @@
 
     def second(o, carry):
         send_qkv(1, o)
-        send_cot(2 * o)
-        send_cot(2 * o + 1)
         return carry
 
+    cot_quarters()
     keep_qkv(0)
     lax.fori_loop(1, NSEQ, first, 0)
-    send_cot(1)
+    cot_along_y()
     lax.fori_loop(1, NSEQ, second, 0)
     keep_qkv(1)
-    pltpu.make_async_copy(cot.at[:, quarter(dp)], cots.at[rows_of(place)], cot_recv).start()
-
-    def attend(h, between):
+    cot_along_x()
+
+    contract = (((1,), (1,)), ((), ()))
+
+    def block_at(step):
+        even = lax.rem(step, 2) == 0
+        return lax.rem(z + jnp.where(even, 4 - step // 2, 5 + step // 2), NZ)
+
+    def rows_at(step):
+        return pl.ds(pl.multiple_of(block_at(step) * BLOCK, BLOCK), BLOCK)
+
+    def scores_of(h, rows):
+        return lax.dot_general(
+            qkv[h, 0, rows, :HEAD_DIM], qkv[h, 1, :, :HEAD_DIM], contract,
+            preferred_element_type=jnp.float32,
+        )
+
+    def dprobs_of(h, rows, probs):
+        q = qkv[h, 0, rows, :]
+        dscores = lax.dot_general(
+            jnp.concatenate([q[:, HEAD_DIM:], q[:, :HEAD_DIM]], axis=1), qkv[h, 1], contract,
+            preferred_element_type=jnp.float32,
+        ) * SCALE
+        centre = jnp.sum(probs * dscores, axis=-1, keepdims=True)
+        return (probs * (dscores - centre)).astype(jnp.bfloat16)
+
+    def go_home(source, target, recv, h, step):
+        for y in (0, 1):
+            to = block_at(step) * 2 + y
+
+            @pl.when(to != seq)
+            def _():
+                pltpu.make_async_remote_copy(
+                    source.at[h, rows_of(to)], target.at[:, head_columns(seq, h)],
+                    out_send, recv, device_id=(dp, to), device_id_type=MESH,
+                ).start()
+
+            @pl.when(to == seq)
+            def _():
+                pltpu.make_async_copy(
+                    source.at[h, rows_of(to)], target.at[:, head_columns(seq, h)], recv
+                ).start()
+
+    def primal_home(h, step):
+        go_home(own, att_out, att_recv.at[h, seq], h, step)
+
+    def tangent_home(h, step):
+        go_home(own_t, tan_out, tan_recv, h, step)
+
+    def attend(h, step):
+        rows = rows_at(step)
+        scores = scores_of(h, rows)
+        top = jnp.max(scores, axis=-1, keepdims=True)
+        expo = jnp.exp((scores - top) * SCALE)
+        probs = expo * (1.0 / jnp.sum(expo, axis=-1, keepdims=True))
+        dprobs = dprobs_of(h, rows, probs)
+        both = jnp.dot(
+            probs.astype(jnp.bfloat16), qkv[h, 2], preferred_element_type=jnp.float32
+        )
+        dout = both[:, HEAD_DIM:] + jnp.dot(
+            dprobs, qkv[h, 2, :, :HEAD_DIM], preferred_element_type=jnp.float32
+        )
+        own[h, rows, :] = both[:, :HEAD_DIM].astype(jnp.bfloat16)
+        own_t[h, rows, :] = dout.astype(jnp.bfloat16)
+
+    def attend_primal(h, step):
+        rows = rows_at(step)
+        scores = scores_of(h, rows)
+        top = jnp.max(scores, axis=-1, keepdims=True)
+        expo = jnp.exp((scores - top) * SCALE)
+        share = 1.0 / jnp.sum(expo, axis=-1, keepdims=True)
+        out = jnp.dot(
+            (expo * share).astype(jnp.bfloat16), qkv[h, 2, :, :HEAD_DIM],
+            preferred_element_type=jnp.float32,
+        )
+        own[h, rows, :] = out.astype(jnp.bfloat16)
+        stats[rows, 0:1] = top
+        stats[rows, 1:2] = share
+
+    def attend_tangent(h, step):
+        rows = rows_at(step)
+        probs = jnp.exp((scores_of(h, rows) - stats[rows, 0:1]) * SCALE) * stats[rows, 1:2]
+        dprobs = dprobs_of(h, rows, probs)
+        dout = jnp.dot(
+            probs.astype(jnp.bfloat16), qkv[h, 2, :, HEAD_DIM:],
+            preferred_element_type=jnp.float32,
+        ) + jnp.dot(dprobs, qkv[h, 2, :, :HEAD_DIM], preferred_element_type=jnp.float32)
+        own_t[h, rows, :] = dout.astype(jnp.bfloat16)
+
+    def steps(h, start, stop, *parts):
         def one(step, carry):
-            even = lax.rem(step, 2) == 0
-            b = lax.rem(z + jnp.where(even, 4 - step // 2, 5 + step // 2), NZ)
-            rows = pl.ds(pl.multiple_of(b * BLOCK, BLOCK), BLOCK)
-            q = qkv[h, 0, rows, :]
-            query, dquery = q[:, :HEAD_DIM], q[:, HEAD_DIM:]
-            contract = (((1,), (1,)), ((), ()))
-            scores = lax.dot_general(
-                query, qkv[h, 1, :, :HEAD_DIM], contract, preferred_element_type=jnp.float32
-            )
-            dscores = lax.dot_general(
-                jnp.concatenate([dquery, query], axis=1), qkv[h, 1], contract,
-                preferred_element_type=jnp.float32,
-            ) * SCALE
-            top = jnp.max(scores, axis=-1, keepdims=True)
-            expo = jnp.exp((scores - top) * SCALE)
-            probs = expo * (1.0 / jnp.sum(expo, axis=-1, keepdims=True))
-            centre = jnp.sum(probs * dscores, axis=-1, keepdims=True)
-            dprobs = (probs * (dscores - centre)).astype(jnp.bfloat16)
-            both = jnp.dot(
-                probs.astype(jnp.bfloat16), qkv[h, 2], preferred_element_type=jnp.float32
-            )
-            dout = both[:, HEAD_DIM:] + jnp.dot(
-                dprobs, qkv[h, 2, :, :HEAD_DIM], preferred_element_type=jnp.float32
-            )
-            own[h, rows, :] = both[:, :HEAD_DIM].astype(jnp.bfloat16)
-            own_t[h, rows, :] = dout.astype(jnp.bfloat16)
-
-            for source, target, recv in (
-                (own, att_out, att_recv.at[h, seq]), (own_t, tan_out, tan_recv)
-            ):
-                for y in (0, 1):
-                    to = b * 2 + y
-
-                    @pl.when(to != seq)
-                    def _():
-                        pltpu.make_async_remote_copy(
-                            source.at[h, rows_of(to)], target.at[:, head_columns(seq, h)],
-                            out_send, recv, device_id=(dp, to), device_id_type=MESH,
-                        ).start()
-
-                    @pl.when(to == seq)
-                    def _():
-                        pltpu.make_async_copy(
-                            source.at[h, rows_of(to)], target.at[:, head_columns(seq, h)], recv
-                        ).start()
-
-            for at, what in between:
-                @pl.when(step == at)
-                def _():
-                    what()
-
+            for part in parts:
+                part(h, step)
             return carry
 
-        lax.fori_loop(0, BLOCKS, one, 0)
+        lax.fori_loop(start, stop, one, 0)
 
     def spread(h):
         def one(o, carry):
@@ -217,14 +277,14 @@
                 def _():
                     pltpu.make_async_copy(
                         att_out.at[:, head_columns(source, h)],
-                        atts.at[h, rows_of(place), lanes], spread_recv.at[h],
+                        atts.at[h, place // 2, c, :, lanes], spread_recv.at[h],
                     ).start()
 
                 @pl.when(jnp.logical_not(is_here))
                 def _():
                     pltpu.make_async_remote_copy(
                         att_out.at[:, head_columns(source, h)],
-                        atts.at[h, rows_of(place), lanes],
+                        atts.at[h, place // 2, c, :, lanes],
                         spread_send.at[h], spread_recv.at[h],
                         device_id=(dp_to, seq_to), device_id_type=MESH,
                     ).start()
@@ -233,27 +293,26 @@
 
         lax.fori_loop(0, NSEQ, one, 0)
 
-    def core_rows(core):
-        return pl.ds(pl.multiple_of(core * (PLANE_TOKENS // 2), 128), PLANE_TOKENS // 2)
-
     def exchange(h):
-        wait_bytes(atts.at[h, core_rows(c)], spread_recv.at[h])
+        wait_bytes(atts.at[h, :, c], spread_recv.at[h])
         pltpu.make_async_remote_copy(
-            atts.at[h, core_rows(c)], atts.at[h, core_rows(c)], core_send.at[h],
+            atts.at[h, :, c], atts.at[h, :, c], core_send.at[h],
             core_recv.at[h], device_id=(dp + 1 - 2 * c, seq), device_id_type=MESH,
         ).start()
 
     def weigh(h):
-        wait_bytes(atts.at[h, core_rows(1 - c)], core_recv.at[h])
+        wait_bytes(atts.at[h, :, 1 - c], core_recv.at[h])
         span = 1024
 
         def one(n, carry):
             tokens = pl.ds(pl.multiple_of(n * span, span), span)
             product = lax.dot_general(
-                cots[tokens, :], atts[h, tokens, :], (((0,), (0,)), ((), ())),
+                cots[tokens, :], atts[h, pl.ds(n * 4, 4)].reshape(span, 256), (((0,), (0,)), ((), ())),
                 preferred_element_type=jnp.float32,
             )
-            term[h] = jnp.where(n == 0, product, term[h] + product)
+            total = jnp.where(n == 0, product, total_of[...] + product)
+            total_of[...] = total
+            term[h] = total.astype(jnp.bfloat16)
             return carry
 
         lax.fori_loop(0, PLANE_TOKENS // span, one, 0)
@@ -287,30 +346,40 @@
 
     def total(h):
         wait_bytes(terms.at[h], term_recv.at[h])
-        result = terms[h, 0]
+        result = terms[h, 0].astype(jnp.float32)
         for s in range(1, NZ):
-            result = result + terms[h, s]
+            result = result + terms[h, s].astype(jnp.float32)
         wg_out[:, pl.ds(h * 128, 128)] = result
 
     wait_bytes(qkv.at[0], qkv_recv.at[0])
-    attend(0, ())
+    steps(0, 0, BLOCKS, attend, primal_home)
     wait_bytes(qkv.at[1], qkv_recv.at[1])
-    attend(1, ((4, lambda: spread(0)), (6, lambda: exchange(0))))
+    steps(0, 0, BLOCKS, tangent_home)
+    steps(1, 0, BLOCKS, attend_primal, primal_home)
+    spread(0)
+    steps(1, 0, 3, attend_tangent, tangent_home)
+    exchange(0)
     spread(1)
-    wait_bytes(cots, cot_recv)
+    steps(1, 3, 6, attend_tangent, tangent_home)
+    for n in range(3):
+        wait_bytes(cots.at[same_x], cot_recv.at[5 + n])
     weigh(0)
     exchange(1)
+    steps(1, 6, BLOCKS, attend_tangent, tangent_home)
     weigh(1)
     total(0)
     total(1)
 
     wait_bytes(tan_out, tan_recv)
     sent = pl.ds(0, (NSEQ - 1) * TOKENS)
-    wait_bytes(cots.at[pl.ds(0, (PLANE - 1) * TOKENS)], cot_send)
+    for n in range(3):
+        wait_bytes(cots.at[rows_of(place)], cot_send.at[n])
+        wait_bytes(cots.at[same_x], cot_send.at[4 + n])
+    wait_bytes(cots.at[same_y], cot_send.at[3])
     for h in range(LOCAL_HEADS):
         wait_bytes(qkv.at[h, :, sent], qkv_send.at[h])
-        wait_bytes(atts.at[h, pl.ds(0, 15 * TOKENS)], spread_send.at[h])
-        wait_bytes(atts.at[h, core_rows(c)], core_send.at[h])
+        wait_bytes(atts.at[h, pl.ds(0, 15), c], spread_send.at[h])
+        wait_bytes(atts.at[h, :, c], core_send.at[h])
 
         @pl.when(mine)
         def _():
@@ -343,10 +412,12 @@
             pltpu.VMEM((PLANE_TOKENS, QUARTER), bf16),
             pltpu.VMEM((LOCAL_HEADS, SEQ_LEN, HEAD_DIM), bf16),
             pltpu.VMEM((LOCAL_HEADS, SEQ_LEN, HEAD_DIM), bf16),
-            pltpu.VMEM((LOCAL_HEADS, PLANE_TOKENS, 256), bf16),
-            pltpu.VMEM((LOCAL_HEADS, QUARTER, 256), f32),
-            pltpu.VMEM((LOCAL_HEADS, NZ, ROWS, HEAD_DIM), f32),
-            dma((2,)), dma((2,)), dma(()), dma(()), dma(()), dma((2, NSEQ)), dma(()),
+            pltpu.VMEM((SEQ_LEN, HEAD_DIM), f32),
+            pltpu.VMEM((LOCAL_HEADS, PLANE // 2, 2, TOKENS, 256), bf16),
+            pltpu.VMEM((QUARTER, 256), f32),
+            pltpu.VMEM((LOCAL_HEADS, QUARTER, 256), bf16),
+            pltpu.VMEM((LOCAL_HEADS, NZ, ROWS, HEAD_DIM), bf16),
+            dma((2,)), dma((2,)), dma((7,)), dma((8,)), dma(()), dma((2, NSEQ)), dma(()),
             dma((2,)), dma((2,)), dma((2,)), dma((2,)), dma((2,)), dma((2,)),
         ],
         compiler_params=pltpu.CompilerParams(

time: 290 us -> 232 us (0.80)
  Pallas kernels: 279 us -> 222 us
    pallas_call x1, Pallas kernels: 279 us -> 222 us  [body(): pl.pallas_call(kernel, out_shape=(jax.ShapeDtypeStruct((TOKENS, WIDTH), b...]
where the time goes in v3:
time: 232 us; the launch traced here: 228 us
  Pallas kernels  222 us (96%)
  local copies, waits for them, and re-layouts  5.28 us (2%)
    pallas_call x1, Pallas kernels, body(): pl.pallas_call(kernel, out_shape=(jax.ShapeDtypeStruct((TOKENS, WIDTH), b...  222 us
    unnamed x5, local copies, waits for them, and re-layouts  5.28 us

profile of v3, /device:TPU:47, one launch (start us, length us, event | category | flops | bytes accessed | tf_op | source)
XLA Modules:
  0.0 228.2 jit_solution(6018627296292374059)
XLA Ops:
  0.6 222.3 %attention_jvp.1 = (bf16[128,4096]{1,0:T(8,128)(2,1)}, bf16[128,4096]{1,0:T(8,128)(2,1)}, f32[160,256]{1,0:T(8,128)}) custom-call(bf16[3,128,4096]{2,1,0:T(8,128)(2,1)} %bitcast.11, bf16[3,128,4096]{2,1,0:T(8,128)(2,1)} %bitcast.12, bf16[128,2560]{1,0:T(8,128)(2,1)} %bitcast.13), custom_call_target="tpu_custom_call" | custom-call | flops 15569256448 | bytes 16777216 | tf_op jit(solution)/shard_map/attention_jvp/pallas_call | solution.py:401
  222.9 0.0 copy-start
  222.9 2.3 %copy.9 = bf16[1,128,4096]{2,1,0:T(8,128)(2,1)} copy(bf16[1,128,4096]{2,1,0:T(8,128)(2,1)} %bitcast.10) | data formatting | bytes 2097152
  225.3 2.3 %copy.10 = bf16[1,128,4096]{2,1,0:T(8,128)(2,1)} copy(bf16[1,128,4096]{2,1,0:T(8,128)(2,1)} %bitcast.9) | data formatting | bytes 2097152
  227.6 0.0 copy-done
  227.6 0.7 copy.11
Async XLA Ops:
  222.9 4.6 %copy-start = (f32[160,256]{1,0:T(8,128)S(1)}, f32[160,256]{1,0:T(8,128)}, u32[]{:S(2)}) copy-start(f32[160,256]{1,0:T(8,128)} %get-tuple-element.14) | copy-start | bytes 491524

commit v4 on v3

--- a/solution.py
+++ b/solution.py
@@ -352,9 +352,8 @@
         wg_out[:, pl.ds(h * 128, 128)] = result
 
     wait_bytes(qkv.at[0], qkv_recv.at[0])
-    steps(0, 0, BLOCKS, attend, primal_home)
+    steps(0, 0, BLOCKS, attend, primal_home, tangent_home)
     wait_bytes(qkv.at[1], qkv_recv.at[1])
-    steps(0, 0, BLOCKS, tangent_home)
     steps(1, 0, BLOCKS, attend_primal, primal_home)
     spread(0)
     steps(1, 0, 3, attend_tangent, tangent_home)

time: 232 us -> 241 us (1.039)
  the two profiles are of different devices: /device:TPU:47 before, /device:TPU:27 now
where the time goes in v4:
time: 241 us
  Pallas kernels  235 us (98%)
  local copies, waits for them, and re-layouts  5.28 us (2%)
    pallas_call x1, Pallas kernels, body(): pl.pallas_call(kernel, out_shape=(jax.ShapeDtypeStruct((TOKENS, WIDTH), b...  235 us
    unnamed x5, local copies, waits for them, and re-layouts  5.28 us

profile of v4, /device:TPU:27, one launch (start us, length us, event | category | flops | bytes accessed | tf_op | source)
XLA Modules:
  0.0 241.1 jit_solution(12669651295416778857)
XLA Ops:
  0.6 235.1 %attention_jvp.1 = (bf16[128,4096]{1,0:T(8,128)(2,1)}, bf16[128,4096]{1,0:T(8,128)(2,1)}, f32[160,256]{1,0:T(8,128)}) custom-call(bf16[3,128,4096]{2,1,0:T(8,128)(2,1)} %bitcast.11, bf16[3,128,4096]{2,1,0:T(8,128)(2,1)} %bitcast.12, bf16[128,2560]{1,0:T(8,128)(2,1)} %bitcast.13), custom_call_target="tpu_custom_call" | custom-call | flops 15569256448 | bytes 16777216 | tf_op jit(solution)/shard_map/attention_jvp/pallas_call | solution.py:400
  235.8 0.0 copy-start
  235.8 2.3 copy.9
  238.1 2.3 copy.10
  240.4 0.0 copy-done
  240.4 0.7 copy.11
Async XLA Ops:
  235.8 4.6 %copy-start = (f32[160,256]{1,0:T(8,128)S(1)}, f32[160,256]{1,0:T(8,128)}, u32[]{:S(2)}) copy-start(f32[160,256]{1,0:T(8,128)} %get-tuple-element.14) | copy-start | bytes 491524
